TPU v7x, 32 devices: a whole 2x2x4 slice. The times are simulated.
32 devices in a mesh: grp: 2 (over y), ep: 16 (over z, x, core).
Axes of the slice: x: 2, y: 2, z: 4, core: 2. Of those that a mesh axis runs over, the one named last changes fastest.
Arguments:
- resid: bfloat16 [96, 7168], P(('grp', 'ep')), parts along dimension 0, may hold values from -24 to 24
- q_latent: bfloat16 [96, 64, 512], P(('grp', 'ep')), parts along dimension 0, may hold values from -96 to 96
- q_rope: bfloat16 [96, 64, 64], P(('grp', 'ep')), parts along dimension 0, may hold values from -6 to 6
- cache_latent: bfloat16 [96, 512, 512], P(('grp', 'ep')), parts along dimension 0, may hold values from -6 to 6
- cache_rope: bfloat16 [96, 512, 64], P(('grp', 'ep')), parts along dimension 0, may hold values from -6 to 6
- lengths: int32 [96], P(('grp', 'ep')), parts along dimension 0, may hold values from 2 to 512, as said below
- proj_weight: bfloat16 [32768, 7168], P('ep'), may hold values from -0.1875 to 0.1875
- norm_gain: float32 [7168], replicated, may hold values from 0.1 to 1.9
- expert_ids: int32 [96, 2], P(('grp', 'ep')), parts along dimension 0, may hold values from 0 to 1, all different within a row; in each aligned block of 3 rows (0 to 2, 3 to 5, ...) at most 3 rows name the same one
- affinity: float32 [96, 2], P(('grp', 'ep')), parts along dimension 0, may hold values from 0.05 to 1
- w_gate: bfloat16 [16, 7168, 128], P('ep'), may hold values from -0.0625 to 0.0625
- w_up: bfloat16 [16, 7168, 128], P('ep'), may hold values from -0.0625 to 0.0625
- w_down: bfloat16 [16, 128, 7168], P('ep'), may hold values from -0.1875 to 0.1875
Outputs:
- mixed: bfloat16 [96, 7168], P(('grp', 'ep')), parts along dimension 0
There are 2 independent parts, one for each index of `grp`. A program takes and returns all parts, laid end to end along the dimension named above; an argument that names none is the same for every part. Nothing has to cross between parts.
Inputs may be any that keep to these rules, and one draw needn't show every extreme that they name: `expert_ids`: among the 3 rows of one device (aligned blocks) no expert is named more than 3 times, a bound that some block reaches; a row names 2 different experts. `lengths`: in every draw some sequence uses all 512 positions.
All inputs are finite; a program needn't handle non-finite values.
Results may differ from a plain program's by a relative error of at most 0.0075.
Values may be sent and summed in bfloat16 or wider, within the bound.
A program may use at most 128 MiB of HBM per device.

v0:
```python
import jax
import jax.numpy as jnp
from jax import lax
from jax.sharding import PartitionSpec as P

SPLIT = 8
CAP = 3


score_scale = 0.07216878364870322
route_factor = 2.5
norm_eps = 1e-06


def partner(value, axis, stride):
    mask = 2**stride
    pairs = [(source, source ^ mask) for source in range(lax.axis_size(axis))]
    return lax.ppermute(value, axis, pairs)


def local(
    resid,
    q_latent,
    q_rope,
    cache_latent,
    cache_rope,
    lengths,
    proj_weight,
    norm_gain,
    expert_ids,
    affinity,
    w_gate,
    w_up,
    w_down,
):
    seq_count = resid.shape[0]
    model_width = resid.shape[1]
    ctx_len = cache_latent.shape[1]
    topk_count = expert_ids.shape[1]
    devices = lax.axis_size("ep")
    experts_all = devices // SPLIT
    scores = jnp.einsum("thc,tlc->thl", q_latent, cache_latent, preferred_element_type=jnp.float32)
    scores = (
        scores + jnp.einsum("thr,tlr->thl", q_rope, cache_rope, preferred_element_type=jnp.float32)
    ) * score_scale
    positions = jnp.arange(ctx_len, dtype=jnp.int32)
    valid_mask = positions[None, None, :] < lengths[:, None, None]
    scores = jnp.where(valid_mask, scores, -1e30)
    peak_score = jnp.max(scores, axis=2, keepdims=True)
    exponent = jnp.where(valid_mask, jnp.exp(scores - peak_score), 0.0)
    attention_weight = (exponent / jnp.sum(exponent, axis=2, keepdims=True)).astype(jnp.bfloat16)
    heads_out = jnp.einsum(
        "thl,tlc->thc", attention_weight, cache_latent, preferred_element_type=jnp.float32
    ).astype(jnp.bfloat16)
    flat_heads = heads_out.reshape(seq_count, -1)
    incoming = lax.all_to_all(flat_heads, "ep", split_axis=1, concat_axis=0, tiled=True)
    row_block = incoming
    attention = lax.psum_scatter(
        jnp.dot(row_block, proj_weight, preferred_element_type=jnp.float32),
        "ep",
        scatter_dimension=0,
        tiled=True,
    )
    hidden = resid.astype(jnp.float32) + attention
    normed = (
        hidden * lax.rsqrt(jnp.mean(hidden * hidden, axis=1, keepdims=True) + norm_eps) * norm_gain
    ).astype(jnp.bfloat16)
    route_weight = route_factor * affinity / jnp.sum(affinity, axis=1, keepdims=True)
    flat_ids = expert_ids.reshape(-1)
    expert_cols = jnp.arange(experts_all, dtype=jnp.int32)
    onehot = (flat_ids[:, None] == expert_cols[None, :]).astype(jnp.int32)
    rank_before = jnp.cumsum(onehot, axis=0) - onehot
    slot_index = jnp.sum(rank_before * onehot, axis=1)
    target = flat_ids * CAP + slot_index
    slot_cols = jnp.arange(experts_all * CAP, dtype=jnp.int32)
    picker = (target[:, None] == slot_cols[None, :]).astype(jnp.bfloat16)
    repeated = jnp.repeat(normed, topk_count, axis=0)
    packed = jnp.einsum("as,ad->sd", picker, repeated, preferred_element_type=jnp.float32).astype(
        jnp.bfloat16
    )
    outgoing = jnp.broadcast_to(
        packed.reshape(experts_all, 1, CAP, model_width), (experts_all, SPLIT, CAP, model_width)
    )
    outgoing = outgoing.reshape(devices, CAP, model_width)
    arrived = lax.all_to_all(outgoing, "ep", split_axis=0, concat_axis=0, tiled=True)
    item_count = arrived.shape[1]
    row_block = arrived.reshape(devices * item_count, model_width)
    gate_val = jnp.dot(row_block, w_gate[0], preferred_element_type=jnp.float32)
    up_val = jnp.dot(row_block, w_up[0], preferred_element_type=jnp.float32)
    active = (jax.nn.silu(gate_val) * up_val).astype(jnp.bfloat16)
    partial_value = jnp.dot(active, w_down[0], preferred_element_type=jnp.float32).reshape(
        devices, item_count, model_width
    )
    position = lax.axis_index("ep")
    levels = SPLIT.bit_length() - 1
    for level_bit in range(levels - 1, -1, -1):
        half_width = partial_value.shape[2] // 2
        lower_half = partial_value[:, :, :half_width]
        upper_half = partial_value[:, :, half_width:]
        upper_side = position >> level_bit & 1 == 1
        keeper = jnp.where(upper_side, upper_half, lower_half)
        leaving = jnp.where(upper_side, lower_half, upper_half)
        partial_value = keeper + partner(leaving, "ep", level_bit)
    arrived_back = lax.all_to_all(
        partial_value.astype(jnp.bfloat16), "ep", split_axis=0, concat_axis=0, tiled=True
    )
    expert_out = arrived_back.reshape(experts_all, SPLIT, CAP, model_width // SPLIT).transpose(
        0, 2, 1, 3
    )
    expert_out = expert_out.reshape(experts_all * CAP, model_width)
    picked = jnp.dot(picker, expert_out, preferred_element_type=jnp.float32).reshape(
        seq_count, topk_count, model_width
    )
    mixture = jnp.sum(route_weight[:, :, None] * picked, axis=1)
    return (hidden + mixture).astype(jnp.bfloat16)


def solution(mesh):
    placed = (
        P(("grp", "ep"), None),
        P(("grp", "ep"), None, None),
        P(("grp", "ep"), None, None),
        P(("grp", "ep"), None, None),
        P(("grp", "ep"), None, None),
        P(("grp", "ep")),
        P("ep", None),
        P(),
        P(("grp", "ep"), None),
        P(("grp", "ep"), None),
        P("ep", None, None),
        P("ep", None, None),
        P("ep", None, None),
    )
    return jax.shard_map(
        local, mesh=mesh, in_specs=placed, out_specs=P(("grp", "ep"), None), check_vma=False
    )
```

profile of v0, /device:TPU:0, one launch (start us, length us, event | category | flops | bytes accessed | tf_op | source)
XLA Modules:
  0.0 226.7 jit_solution(10254134875778733199)
XLA Ops:
  6.5 0.9 iota_compare_fusion
  7.4 2.2 fusion.29
  9.7 0.2 fusion.10
  9.9 0.7 copy-done.5
  10.6 0.2 fusion.28
  10.8 2.2 convolution_convert_fusion.1
  13.0 1.1 all_to_all.20
  14.1 0.2 copy.32
  14.3 17.2 %all_to_all.29 = bf16[3,16,2048]{2,0,1:T(4,128)(2,1)S(1)} all-to-all(bf16[3,16,2048]{2,0,1:T(4,128)(2,1)S(1)} %copy.32), channel_id=1, replica_groups=mesh['grp'=2,'ep'=16] {'ep'}, dimensions={1} | all-to-all | bytes 393216 | tf_op jit(solution)/shard_map/all_to_all | solution.py:56
  31.5 0.2 all_to_all.23
  31.7 0.0 copy-start.11
  31.7 13.1 %fusion.30 = f32[48,7168]{1,0:T(8,128)} fusion(bf16[48,2048]{1,0:T(8,128)(2,1)S(1)} %all_to_all.23, bf16[2048,7168]{1,0:T(8,128)(2,1)} %param.19), kind=kOutput, calls=%fused_computation.50 | convolution fusion | flops 1409286144 | bytes 30932992 | tf_op jit(solution)/shard_map/dot_general | solution.py:59
  44.8 0.0 all-reduce.3.cloned.1.call-update
  44.9 0.1 copy.33
  45.0 0.1 eq.59
  45.1 0.6 dynamic-slice
  46.3 0.2 reduce_window_sum.11
  46.5 91.4 %all-reduce.3.cloned.1.call-done = f32[48,7168]{1,0:T(8,128)} async-done(((f32[48,7168]{1,0:T(8,128)}), f32[48,7168]{1,0:T(8,128)}) %all-reduce.3.cloned.1.call-update) | async-done | bytes 1376272
  137.9 1.2 multiply_reduce_fusion
  139.1 1.1 multiply_convert_fusion
  140.3 0.1 broadcast_in_dim.42
  140.4 0.3 convolution_convert_fusion
  140.7 0.1 broadcast_in_dim.43
  140.7 1.2 broadcast_in_dim.44
  141.9 3.6 %all-to-all-start.1 = ((bf16[16,3,7168]{2,1,0:T(4,128)(2,1)}), bf16[16,3,7168]{2,1,0:T(4,128)(2,1)S(1)}, u32[]{:S(2)}, u32[]{:S(2)}) async-start(bf16[16,3,7168]{2,1,0:T(4,128)(2,1)} %bitcast.39), calls=%async_computation.1 | async-start | bytes 1835008 | tf_op jit(solution)/shard_map/all_to_all | solution.py:85
  145.6 20.8 %all-to-all-done.1 = bf16[16,3,7168]{2,1,0:T(4,128)(2,1)S(1)} async-done(((bf16[16,3,7168]{2,1,0:T(4,128)(2,1)}), bf16[16,3,7168]{2,1,0:T(4,128)(2,1)S(1)}, u32[]{:S(2)}, u32[]{:S(2)}) %all-to-all-start.1) | async-done | bytes 688160 | tf_op jit(solution)/shard_map/all_to_all | solution.py:85
  166.4 0.6 reshape.95
  167.0 2.1 fusion.5
  169.1 0.4 fusion.16
  169.5 0.4 fusion.1
  169.9 1.0 slice_select_fusion
  170.9 2.7 %collective-permute-start = (f32[16,3,3584]{2,0,1:T(8,128)}, f32[16,3,3584]{2,0,1:T(8,128)}, u32[]{:S(2)}, u32[]{:S(2)}) collective-permute-start(f32[16,3,3584]{2,0,1:T(8,128)} %slice_select_fusion), channel_id=1, source_target_pairs={{0,4},{1,5},{2,6},{3,7},{4,0},{5,1},{6,2},{7,3},{8,12},{9,13},{10,... | collective-permute-start | bytes 2064392 | tf_op jit(solution)/shard_map/ppermute | solution.py:18
  173.6 16.5 %collective-permute-done = f32[16,3,3584]{2,0,1:T(8,128)} collective-permute-done((f32[16,3,3584]{2,0,1:T(8,128)}, f32[16,3,3584]{2,0,1:T(8,128)}, u32[]{:S(2)}, u32[]{:S(2)}) %collective-permute-start) | collective-permute-done | bytes 688160 | tf_op jit(solution)/shard_map/ppermute | solution.py:18
  190.1 1.2 select_add_fusion
  191.3 0.9 copy-done.1
  192.2 1.5 collective-permute-start.1
  193.8 0.1 reduce_sum.50
  193.9 8.5 %collective-permute-done.1 = f32[16,3,1792]{2,0,1:T(8,128)S(1)} collective-permute-done((f32[16,3,1792]{2,0,1:T(8,128)S(1)}, f32[16,3,1792]{2,0,1:T(8,128)S(1)}, u32[]{:S(2)}, u32[]{:S(2)}) %collective-permute-start.1) | collective-permute-done | bytes 344096 | tf_op jit(solution)/shard_map/ppermute | solution.py:18
  202.4 1.1 select_add_fusion.1
  203.6 0.1 collective-permute-start.2
  203.7 0.1 copy.35
  203.8 1.3 collective-permute-done.2
  205.1 0.7 copy.37
  205.8 4.3 %all-to-all-start.2 = ((bf16[16,3,896]{2,1,0:T(4,128)(2,1)}), bf16[16,3,896]{2,1,0:T(4,128)(2,1)S(1)}, u32[]{:S(2)}, u32[]{:S(2)}) async-start(bf16[16,3,896]{2,1,0:T(4,128)(2,1)} %copy.37), calls=%async_computation.2 | async-start | bytes 229376 | tf_op jit(solution)/shard_map/all_to_all | solution.py:104
  210.1 7.7 %all-to-all-done.2 = bf16[16,3,896]{2,1,0:T(4,128)(2,1)S(1)} async-done(((bf16[16,3,896]{2,1,0:T(4,128)(2,1)}), bf16[16,3,896]{2,1,0:T(4,128)(2,1)S(1)}, u32[]{:S(2)}, u32[]{:S(2)}) %all-to-all-start.2) | async-done | bytes 86048 | tf_op jit(solution)/shard_map/all_to_all | solution.py:104
  217.8 0.1 reshape.99
  217.9 0.3 fusion.12
  218.2 1.7 add_convert_fusion.1
  (35 shorter events, 0.3 us)
Async XLA Ops:
  6.5 163.0 %copy-start = (bf16[1,128,7168]{2,1,0:T(8,128)(2,1)S(1)}, bf16[1,128,7168]{2,1,0:T(8,128)(2,1)}, u32[]{:S(2)}) copy-start(bf16[1,128,7168]{2,1,0:T(8,128)(2,1)} %param.25) | copy-start | bytes 5505028
  6.5 3.1 %copy-start.7 = (bf16[3,64,64]{2,1,0:T(8,128)(2,1)S(1)}, bf16[3,64,64]{2,1,0:T(8,128)(2,1)}, u32[]{:S(2)}) copy-start(bf16[3,64,64]{2,1,0:T(8,128)(2,1)} %param.15) | copy-start | bytes 73732
  6.5 131.4 %all-reduce.3.cloned.1.call-start = ((), (), s32[]{:S(2)}) async-start(), calls=%async_computation.3 | async-start | bytes 2752512
  6.5 3.1 %copy-start.6 = (bf16[3,512,64]{1,2,0:T(8,128)(2,1)S(1)}, bf16[3,512,64]{1,2,0:T(8,128)(2,1)}, u32[]{:S(2)}) copy-start(bf16[3,512,64]{1,2,0:T(8,128)(2,1)} %param.17) | copy-start | bytes 589828
  7.4 3.4 %copy-start.3 = (bf16[3,512,512]{2,1,0:T(8,128)(2,1)S(1)}, bf16[3,512,512]{2,1,0:T(8,128)(2,1)}, u32[]{:S(2)}) copy-start(bf16[3,512,512]{2,1,0:T(8,128)(2,1)} %param.16) | copy-start | bytes 4718596
  9.8 0.7 copy-start.5
  31.6 13.2 %copy-start.10 = (s32[3,2]{0,1:T(2,128)S(1)}, s32[3,2]{0,1:T(2,128)}, u32[]{:S(2)}) copy-start(s32[3,2]{0,1:T(2,128)} %param.21) | copy-start | bytes 76
  31.7 13.4 %copy-start.11 = (u32[32]{0:T(128)S(1)}, u32[32]{0:T(128)}, u32[]{:S(2)}) copy-start(u32[32]{0:T(128)} %constant.47) | copy-start | bytes 388
  31.7 106.3 %copy-start.4 = (bf16[3,7168]{1,0:T(4,128)(2,1)S(1)}, bf16[3,7168]{1,0:T(4,128)(2,1)}, u32[]{:S(2)}) copy-start(bf16[3,7168]{1,0:T(4,128)(2,1)} %param.13) | copy-start | bytes 129028
  44.8 94.3 %copy-start.8 = (f32[7168]{0:T(1024)S(1)}, f32[7168]{0:T(1024)}, u32[]{:S(2)}) copy-start(f32[7168]{0:T(1024)} %param.20) | copy-start | bytes 86020
  141.9 24.4 %all-to-all-start.1 = ((bf16[16,3,7168]{2,1,0:T(4,128)(2,1)}), bf16[16,3,7168]{2,1,0:T(4,128)(2,1)S(1)}, u32[]{:S(2)}, u32[]{:S(2)}) async-start(bf16[16,3,7168]{2,1,0:T(4,128)(2,1)} %bitcast.39), calls=%async_computation.1 | async-start | bytes 1835008 | tf_op jit(solution)/shard_map/all_to_all | solution.py:85
  167.0 2.1 copy-start.2
  170.9 19.2 %collective-permute-start = (f32[16,3,3584]{2,0,1:T(8,128)}, f32[16,3,3584]{2,0,1:T(8,128)}, u32[]{:S(2)}, u32[]{:S(2)}) collective-permute-start(f32[16,3,3584]{2,0,1:T(8,128)} %slice_select_fusion), channel_id=1, source_target_pairs={{0,4},{1,5},{2,6},{3,7},{4,0},{5,1},{6,2},{7,3},{8,12},{9,13},{10,... | collective-permute-start | bytes 2064392 | tf_op jit(solution)/shard_map/ppermute | solution.py:18
  191.3 0.9 copy-start.1
  192.2 11.5 %copy-start.9 = (f32[3,2]{0,1:T(2,128)S(1)}, f32[3,2]{0,1:T(2,128)}, u32[]{:S(2)}) copy-start(f32[3,2]{0,1:T(2,128)} %param.22) | copy-start | bytes 76
  192.2 10.1 %collective-permute-start.1 = (f32[16,3,1792]{2,0,1:T(8,128)S(1)}, f32[16,3,1792]{2,0,1:T(8,128)S(1)}, u32[]{:S(2)}, u32[]{:S(2)}) collective-permute-start(f32[16,3,1792]{2,0,1:T(8,128)S(1)} %slice_select_fusion.1), channel_id=1, source_target_pairs={{0,2},{1,3},{2,0},{3,1},{4,6},{5,7},{6,4},{7,5},{8,10},{9,11},{10,... | collective-permute-start | bytes 1032200 | tf_op jit(solution)/shard_map/ppermute | solution.py:18
  203.6 1.5 collective-permute-start.2
  205.8 12.0 %all-to-all-start.2 = ((bf16[16,3,896]{2,1,0:T(4,128)(2,1)}), bf16[16,3,896]{2,1,0:T(4,128)(2,1)S(1)}, u32[]{:S(2)}, u32[]{:S(2)}) async-start(bf16[16,3,896]{2,1,0:T(4,128)(2,1)} %copy.37), calls=%async_computation.2 | async-start | bytes 229376 | tf_op jit(solution)/shard_map/all_to_all | solution.py:104
Sparse Core Ops, SparseCore 0:
  45.0 92.9 all-reduce.2
where the time goes:
time: 227 us
  waiting for transfers between devices  146 us (64%)
  matrix products  21.2 us (9%)
  blocking collectives  17.2 us (8%)
  between operations  14.3 us (6%)
  starting transfers between devices  12.2 us (5%)
  other arithmetic  8.76 us (4%)
  local copies, waits for them, and re-layouts  6.79 us (3%)
    unnamed x2, waiting for transfers between devices  91.4 us
    ppermute x3, waiting for transfers between devices, partner(): return lax.ppermute(value, axis, pairs)  26.3 us
    all_to_all x1, waiting for transfers between devices, local(): lax.all_to_all(outgoing, 'ep', split_axis=0, concat_axis=0, tiled=True)  20.8 us
    all_to_all x1, blocking collectives, local(): lax.all_to_all(flat_heads, 'ep', split_axis=1, concat_axis=0, tiled=True)  17.2 us
    dot_general x1, matrix products, local(): jnp.dot(row_block, proj_weight, preferred_element_type=jnp.float32)  13.1 us
    all_to_all x1, waiting for transfers between devices, local(): lax.all_to_all(partial_value.astype(jnp.bfloat16), 'ep', split_axis=0, co...  7.66 us
  transfers between devices with their start and end apart: 6, of which 6 were waited for; matrix products, arithmetic and copies ran while one was open for 1% of the time, Pallas kernels for 0%

commit v1 on v0

v1 whole, which is shorter than its diff:
```python
import jax
import jax.numpy as jnp
from jax import lax
from jax.sharding import PartitionSpec as P

SPLIT = 8


score_scale = 0.07216878364870322
route_factor = 2.5
norm_eps = 1e-06


def scatter_sum(partial):
    devices = lax.axis_size("ep")
    blocks = partial.astype(jnp.bfloat16).reshape(devices, -1, partial.shape[1])
    arrived = lax.all_to_all(blocks, "ep", split_axis=0, concat_axis=0, tiled=True)
    return jnp.sum(arrived.astype(jnp.float32), axis=0)


def local(
    resid,
    q_latent,
    q_rope,
    cache_latent,
    cache_rope,
    lengths,
    proj_weight,
    norm_gain,
    expert_ids,
    affinity,
    w_gate,
    w_up,
    w_down,
):
    seq_count = resid.shape[0]
    ctx_len = cache_latent.shape[1]
    devices = lax.axis_size("ep")
    experts_all = devices // SPLIT
    route_weight = route_factor * affinity / jnp.sum(affinity, axis=1, keepdims=True)
    expert_cols = jnp.arange(experts_all, dtype=jnp.int32)
    named = expert_ids[:, :, None] == expert_cols
    spread = jnp.sum(jnp.where(named, route_weight[:, :, None], 0.0), axis=1)
    spread = lax.all_to_all(
        jnp.repeat(spread.T, SPLIT, axis=0), "ep", split_axis=0, concat_axis=0, tiled=True
    )
    coeff = spread.reshape(-1)
    chosen = coeff != 0.0
    scores = jnp.einsum("thc,tlc->thl", q_latent, cache_latent, preferred_element_type=jnp.float32)
    scores = (
        scores + jnp.einsum("thr,tlr->thl", q_rope, cache_rope, preferred_element_type=jnp.float32)
    ) * score_scale
    positions = jnp.arange(ctx_len, dtype=jnp.int32)
    valid_mask = positions[None, None, :] < lengths[:, None, None]
    scores = jnp.where(valid_mask, scores, -1e30)
    peak_score = jnp.max(scores, axis=2, keepdims=True)
    exponent = jnp.where(valid_mask, jnp.exp(scores - peak_score), 0.0)
    attention_weight = (exponent / jnp.sum(exponent, axis=2, keepdims=True)).astype(jnp.bfloat16)
    heads_out = jnp.einsum(
        "thl,tlc->thc", attention_weight, cache_latent, preferred_element_type=jnp.float32
    ).astype(jnp.bfloat16)
    flat_heads = heads_out.reshape(seq_count, -1)
    incoming = lax.all_to_all(flat_heads, "ep", split_axis=1, concat_axis=0, tiled=True)
    row_block = incoming
    attention = scatter_sum(jnp.dot(row_block, proj_weight, preferred_element_type=jnp.float32))
    hidden = resid.astype(jnp.float32) + attention
    normed = (
        hidden * lax.rsqrt(jnp.mean(hidden * hidden, axis=1, keepdims=True) + norm_eps) * norm_gain
    ).astype(jnp.bfloat16)
    row_block = lax.all_gather(normed, "ep", axis=0, tiled=True)
    gate_val = jnp.dot(row_block, w_gate[0], preferred_element_type=jnp.float32)
    up_val = jnp.dot(row_block, w_up[0], preferred_element_type=jnp.float32)
    active = (jax.nn.silu(gate_val) * up_val).astype(jnp.bfloat16)
    partial_value = jnp.dot(active, w_down[0], preferred_element_type=jnp.float32)
    mixture = scatter_sum(jnp.where(chosen[:, None], partial_value * coeff[:, None], 0.0))
    return (hidden + mixture).astype(jnp.bfloat16)


def solution(mesh):
    placed = (
        P(("grp", "ep"), None),
        P(("grp", "ep"), None, None),
        P(("grp", "ep"), None, None),
        P(("grp", "ep"), None, None),
        P(("grp", "ep"), None, None),
        P(("grp", "ep")),
        P("ep", None),
        P(),
        P(("grp", "ep"), None),
        P(("grp", "ep"), None),
        P("ep", None, None),
        P("ep", None, None),
        P("ep", None, None),
    )
    return jax.shard_map(
        local, mesh=mesh, in_specs=placed, out_specs=P(("grp", "ep"), None), check_vma=False
    )
```

time: 227 us -> 129 us (0.57)
  waiting for transfers between devices: 146 us -> 29 us
  blocking collectives: 17.2 us -> 49.7 us
  between operations: 14.3 us -> 0.24 us
  starting transfers between devices: 12.2 us -> 16.9 us
  other arithmetic: 8.76 us -> 5.16 us
    unnamed x2 -> x0, waiting for transfers between devices: 91.4 us -> none
    ppermute x3 -> x0, waiting for transfers between devices: 26.3 us -> none  [partner(): return lax.ppermute(value, axis, pairs)]
    all_gather x0 -> x1, blocking collectives: none -> 24.5 us  [local(): row_block = lax.all_gather(normed, 'ep', axis=0, tiled=True)]
    all_to_all x2 -> x3, starting transfers between devices: 7.93 us -> 16.9 us  [the longest x1 7.35 us: local(): lax.all_to_all(flat_heads, 'ep', split_axis=1, concat_axis=0, tiled=True)]
    all_to_all x1, blocking collectives: 17.2 us -> 25.3 us  [scatter_sum(): lax.all_to_all(blocks, 'ep', split_axis=0, concat_axis=0, tiled=True)]
    ppermute x3 -> x0, starting transfers between devices: 4.29 us -> none  [partner(): return lax.ppermute(value, axis, pairs)]
    add x4 -> x0, other arithmetic: 2.34 us -> none  [the longest x2 2.33 us: local(): partial_value = keeper + partner(leaving, 'ep', level_bit)]
    all_to_all x2 -> x3, waiting for transfers between devices: 28.4 us -> 29 us  [the longest x1 19 us: scatter_sum(): lax.all_to_all(blocks, 'ep', split_axis=0, concat_axis=0, tiled=True)]
  transfers between devices with their start and end apart: 6 -> 3, of which waited for: 6 -> 2; matrix products, arithmetic and copies ran while one was open for 1% -> 12% of each run, Pallas kernels for 0% -> 0%
where the time goes in v1:
time: 129 us; the launch traced here: 128 us
  blocking collectives  49.7 us (39%)
  waiting for transfers between devices  29 us (22%)
  matrix products  21.7 us (17%)
  starting transfers between devices  16.9 us (13%)
  local copies, waits for them, and re-layouts  5.61 us (4%)
  other arithmetic  5.16 us (4%)
    all_to_all x1, blocking collectives, scatter_sum(): lax.all_to_all(blocks, 'ep', split_axis=0, concat_axis=0, tiled=True)  25.3 us
    all_gather x1, blocking collectives, local(): row_block = lax.all_gather(normed, 'ep', axis=0, tiled=True)  24.5 us
    all_to_all x1, waiting for transfers between devices, scatter_sum(): lax.all_to_all(blocks, 'ep', split_axis=0, concat_axis=0, tiled=True)  19 us
    dot_general x1, matrix products, local(): jnp.dot(row_block, proj_weight, preferred_element_type=jnp.float32)  12.1 us
    all_to_all x1, waiting for transfers between devices, local(): lax.all_to_all(flat_heads, 'ep', split_axis=1, concat_axis=0, tiled=True)  9.98 us
    all_to_all x1, starting transfers between devices, local(): lax.all_to_all(flat_heads, 'ep', split_axis=1, concat_axis=0, tiled=True)  7.35 us
    all_to_all x1, starting transfers between devices, scatter_sum(): lax.all_to_all(blocks, 'ep', split_axis=0, concat_axis=0, tiled=True)  6.11 us
    all_to_all x1, starting transfers between devices, local(): lax.all_to_all(jnp.repeat(spread.T, SPLIT, axis=0), 'ep', split_axis=0, c...  3.47 us
  transfers between devices with their start and end apart: 3, of which 2 were waited for; matrix products, arithmetic and copies ran while one was open for 12% of the time, Pallas kernels for 0%

profile of v1, /device:TPU:0, one launch (start us, length us, event | category | flops | bytes accessed | tf_op | source)
XLA Modules:
  0.0 128.3 jit_solution(7499116301313461364)
XLA Ops:
  0.0 0.0 copy-start
  0.0 0.9 iota_compare_fusion
  0.9 2.2 %fusion.34 = f32[3,64,512]{2,1,0:T(8,128)S(1)} fusion(bf16[3,64,512]{2,1,0:T(8,128)(2,1)} %param.14, bf16[3,512,512]{2,1,0:T(8,128)(2,1)} %param.16), kind=kOutput, calls=%fused_computation.44 | convolution fusion | flops 100663296 | bytes 2162688 | tf_op jit(solution)/shard_map/thc,tlc->thl/dot_general | solution.py:49
  3.1 0.0 copy-done.4
  3.1 0.0 copy-done.5
  3.1 0.9 fusion.11
  4.0 1.3 %fusion.33 = f32[3,64]{1,0:T(4,128)S(1)} fusion(f32[3,64,512]{2,1,0:T(8,128)} %fusion.11, pred[3,512]{1,0:T(4,128)(4,1)S(1)} %iota_compare_fusion), kind=kOutput, calls=%fused_computation.43 | output fusion | flops 295423 | bytes 395520 | tf_op jit(solution)/shard_map/sub | solution.py:57
  5.4 0.0 copy-done.1
  5.4 0.0 copy-start.7
  5.4 0.0 copy-start.10
  5.4 2.2 %convolution_convert_fusion.1 = bf16[3,64,512]{2,1,0:T(8,128)(2,1)} fusion(bf16[3,512,512]{2,1,0:T(8,128)(2,1)S(1)} %copy-done.1, f32[3,64]{1,0:T(4,128)S(1)} %fusion.33, f32[3,64,512]{2,1,0:T(8,128)} %fusion.11, pred[3,512]{1,0:T(4,128)(4,1)S(1)} %iota_compare_fusion), kind=kOutput, calls=%fused_computation.18 | convolution fusion | flops 101155520 | bytes 2164992 | tf_op jit(solution)/shard_map/thl,tlc->thc/dot_general | solution.py:59
  7.7 1.1 all_to_all.26
  8.7 0.9 copy.25
  9.6 7.4 %all-to-all-start = ((bf16[3,16,2048]{2,0,1:T(4,128)(2,1)}), bf16[3,16,2048]{2,0,1:T(4,128)(2,1)S(1)}, u32[]{:S(2)}, u32[]{:S(2)}) async-start(bf16[3,16,2048]{2,0,1:T(4,128)(2,1)} %copy.25), calls=%async_computation | async-start | bytes 524288 | tf_op jit(solution)/shard_map/all_to_all | solution.py:63
  16.9 0.0 copy-done.7
  17.0 0.0 copy-done.10
  17.0 10.0 %all-to-all-done = bf16[3,16,2048]{2,0,1:T(4,128)(2,1)S(1)} async-done(((bf16[3,16,2048]{2,0,1:T(4,128)(2,1)}), bf16[3,16,2048]{2,0,1:T(4,128)(2,1)S(1)}, u32[]{:S(2)}, u32[]{:S(2)}) %all-to-all-start) | async-done | bytes 196640 | tf_op jit(solution)/shard_map/all_to_all | solution.py:63
  27.0 0.6 broadcast_in_dim.61.clone
  27.6 3.5 %all-to-all-start.2 = ((f32[16,1,3]{2,1,0:T(1,128)}), f32[16,1,3]{2,1,0:T(1,128)S(1)}, u32[]{:S(2)}, u32[]{:S(2)}) async-start(f32[16,1,3]{2,1,0:T(1,128)} %bitcast.2), calls=%async_computation.2 | async-start | bytes 16384 | tf_op jit(solution)/shard_map/all_to_all | solution.py:44
  31.1 0.2 all_to_all.29
  31.2 12.1 %convolution_convert_fusion = bf16[48,7168]{1,0:T(8,128)(2,1)S(1)} fusion(bf16[48,2048]{1,0:T(8,128)(2,1)S(1)} %all_to_all.29, bf16[2048,7168]{1,0:T(8,128)(2,1)} %param.19), kind=kOutput, calls=%fused_computation.4 | convolution fusion | flops 1409630208 | bytes 30244864 | tf_op jit(solution)/shard_map/dot_general | solution.py:65
  43.3 1.2 reshape.61
  44.6 0.0 all-to-all-done.2
  44.6 6.1 %all-to-all-start.1 = ((bf16[16,3,7168]{2,1,0:T(4,128)(2,1)}), bf16[16,3,7168]{2,1,0:T(4,128)(2,1)S(1)}, u32[]{:S(2)}, u32[]{:S(2)}) async-start(bf16[16,3,7168]{2,1,0:T(4,128)(2,1)} %reshape.61), calls=%async_computation.1 | async-start | bytes 1835008 | tf_op jit(solution)/shard_map/all_to_all | solution.py:17
  50.7 0.5 broadcast.54
  51.2 0.7 reduce.3
  51.9 0.1 reshape.62
  52.0 0.0 copy-start.8
  52.0 0.5 broadcast_compare_fusion
  52.5 19.0 %all-to-all-done.1 = bf16[16,3,7168]{2,1,0:T(4,128)(2,1)S(1)} async-done(((bf16[16,3,7168]{2,1,0:T(4,128)(2,1)}), bf16[16,3,7168]{2,1,0:T(4,128)(2,1)S(1)}, u32[]{:S(2)}, u32[]{:S(2)}) %all-to-all-start.1) | async-done | bytes 688160 | tf_op jit(solution)/shard_map/all_to_all | solution.py:17
  71.5 0.4 convert_reduce_fusion.1
  71.9 0.0 copy-done.2
  71.9 0.2 multiply_reduce_fusion
  72.1 0.1 fusion.22
  72.2 24.5 %all-gather = bf16[16,3,7168]{2,1,0:T(4,128)(2,1)S(1)} all-gather(bf16[1,3,7168]{2,1,0:T(4,128)(2,1)S(1)} %fusion.22), channel_id=1, replica_groups=mesh['grp'=2,'ep'=16] {'ep'}, dimensions={0}, use_global_device_ids=true | all-gather | bytes 731136 | tf_op jit(solution)/shard_map/all_gather | solution.py:70
  96.7 0.6 reshape.65
  97.3 0.0 copy-start.9
  97.3 0.0 copy-start.11
  97.3 1.9 %fusion.6 = f32[48,128]{1,0:T(8,128)S(1)} fusion(bf16[48,7168]{1,0:T(8,128)(2,1)S(1)} %reshape.65, bf16[1,7168,128]{2,1,0:T(8,128)(2,1)} %param.23), kind=kOutput, calls=%fused_computation.8 | convolution fusion | flops 88080384 | bytes 2547712 | tf_op jit(solution)/shard_map/dot_general | solution.py:71
  99.2 0.0 copy-done
  99.2 0.0 copy-done.9
  99.2 0.0 copy-done.11
  99.3 2.3 %fusion.2 = bf16[48,7168]{1,0:T(8,128)(2,1)S(1)} fusion(bf16[1,128,7168]{2,1,0:T(8,128)(2,1)S(1)} %copy-done, bf16[48,7168]{1,0:T(8,128)(2,1)S(1)} %reshape.65, bf16[1,7168,128]{2,1,0:T(8,128)(2,1)} %param.24, f32[48]{0:T(128)S(1)} %copy-done.9, pred[48]{0:T(512)(128)(4,1)S(1)} %copy-done.11, f32[48,128]{1,0:T(8,128)S(1)} %fusion.6), kind=kOutput, calls=%fused_computation.3 | convolution fusion | flops 177229824 | bytes 5071088 | tf_op jit(solution)/shard_map/dot_general | solution.py:74
  101.5 0.4 reshape.63
  102.0 0.0 copy-start.3
  102.0 25.3 %all_to_all.38 = bf16[16,3,7168]{2,1,0:T(4,128)(2,1)S(1)} all-to-all(bf16[16,3,7168]{2,1,0:T(4,128)(2,1)S(1)} %reshape.63), channel_id=1, replica_groups=mesh['grp'=2,'ep'=16] {'ep'}, dimensions={0} | all-to-all | bytes 1376256 | tf_op jit(solution)/shard_map/all_to_all | solution.py:17
  127.3 0.4 convert_reduce_fusion
  127.7 0.7 add_convert_fusion
  (12 shorter events, 0.1 us)
Async XLA Ops:
  0.0 99.2 %copy-start = (bf16[1,128,7168]{2,1,0:T(8,128)(2,1)S(1)}, bf16[1,128,7168]{2,1,0:T(8,128)(2,1)}, u32[]{:S(2)}) copy-start(bf16[1,128,7168]{2,1,0:T(8,128)(2,1)} %param.25) | copy-start | bytes 5505028
  0.0 3.1 %copy-start.4 = (bf16[3,512,64]{1,2,0:T(8,128)(2,1)S(1)}, bf16[3,512,64]{1,2,0:T(8,128)(2,1)}, u32[]{:S(2)}) copy-start(bf16[3,512,64]{1,2,0:T(8,128)(2,1)} %param.17) | copy-start | bytes 589828
  0.0 3.1 %copy-start.5 = (bf16[3,64,64]{2,1,0:T(8,128)(2,1)S(1)}, bf16[3,64,64]{2,1,0:T(8,128)(2,1)}, u32[]{:S(2)}) copy-start(bf16[3,64,64]{2,1,0:T(8,128)(2,1)} %param.15) | copy-start | bytes 73732
  0.9 4.5 %copy-start.1 = (bf16[3,512,512]{2,1,0:T(8,128)(2,1)S(1)}, bf16[3,512,512]{2,1,0:T(8,128)(2,1)}, u32[]{:S(2)}) copy-start(bf16[3,512,512]{2,1,0:T(8,128)(2,1)} %param.16) | copy-start | bytes 4718596
  5.4 11.5 %copy-start.7 = (f32[3,2]{0,1:T(2,128)S(1)}, f32[3,2]{0,1:T(2,128)}, u32[]{:S(2)}) copy-start(f32[3,2]{0,1:T(2,128)} %param.22) | copy-start | bytes 76
  5.4 11.6 %copy-start.10 = (s32[3,2]{0,1:T(2,128)S(1)}, s32[3,2]{0,1:T(2,128)}, u32[]{:S(2)}) copy-start(s32[3,2]{0,1:T(2,128)} %param.21) | copy-start | bytes 76
  9.6 17.4 %all-to-all-start = ((bf16[3,16,2048]{2,0,1:T(4,128)(2,1)}), bf16[3,16,2048]{2,0,1:T(4,128)(2,1)S(1)}, u32[]{:S(2)}, u32[]{:S(2)}) async-start(bf16[3,16,2048]{2,0,1:T(4,128)(2,1)} %copy.25), calls=%async_computation | async-start | bytes 524288 | tf_op jit(solution)/shard_map/all_to_all | solution.py:63
  27.6 17.0 %all-to-all-start.2 = ((f32[16,1,3]{2,1,0:T(1,128)}), f32[16,1,3]{2,1,0:T(1,128)S(1)}, u32[]{:S(2)}, u32[]{:S(2)}) async-start(f32[16,1,3]{2,1,0:T(1,128)} %bitcast.2), calls=%async_computation.2 | async-start | bytes 16384 | tf_op jit(solution)/shard_map/all_to_all | solution.py:44
  44.6 27.3 %copy-start.2 = (bf16[3,7168]{1,0:T(4,128)(2,1)S(1)}, bf16[3,7168]{1,0:T(4,128)(2,1)}, u32[]{:S(2)}) copy-start(bf16[3,7168]{1,0:T(4,128)(2,1)} %param.13) | copy-start | bytes 129028
  44.6 27.5 %copy-start.6 = (f32[7168]{0:T(1024)S(1)}, f32[7168]{0:T(1024)}, u32[]{:S(2)}) copy-start(f32[7168]{0:T(1024)} %param.20) | copy-start | bytes 86020
  44.6 26.9 %all-to-all-start.1 = ((bf16[16,3,7168]{2,1,0:T(4,128)(2,1)}), bf16[16,3,7168]{2,1,0:T(4,128)(2,1)S(1)}, u32[]{:S(2)}, u32[]{:S(2)}) async-start(bf16[16,3,7168]{2,1,0:T(4,128)(2,1)} %reshape.61), calls=%async_computation.1 | async-start | bytes 1835008 | tf_op jit(solution)/shard_map/all_to_all | solution.py:17
  52.0 20.1 %copy-start.8 = (f32[48]{0:T(128)}, f32[48]{0:T(128)S(1)}, u32[]{:S(2)}) copy-start(f32[48]{0:T(128)S(1)} %reshape.62) | copy-start | bytes 580
  97.3 2.0 %copy-start.9 = (f32[48]{0:T(128)S(1)}, f32[48]{0:T(128)}, u32[]{:S(2)}) copy-start(f32[48]{0:T(128)} %copy-done.8) | copy-start | bytes 580
  97.3 2.0 %copy-start.11 = (pred[48]{0:T(512)(128)(4,1)S(1)}, pred[48]{0:T(512)(128)(4,1)}, u32[]{:S(2)}) copy-start(pred[48]{0:T(512)(128)(4,1)} %broadcast_compare_fusion) | copy-start | bytes 148
  102.0 25.7 %copy-start.3 = (bf16[3,7168]{1,0:T(4,128)(2,1)S(1)}, bf16[3,7168]{1,0:T(4,128)(2,1)}, u32[]{:S(2)}) copy-start(bf16[3,7168]{1,0:T(4,128)(2,1)} %param.13) | copy-start | bytes 129028

commit v2 on v1

--- a/solution.py
+++ b/solution.py
@@ -1,9 +1,15 @@
+import functools
+
 import jax
 import jax.numpy as jnp
 from jax import lax
+from jax.experimental import pallas as pl
+from jax.experimental.pallas import tpu as pltpu
 from jax.sharding import PartitionSpec as P
 
 SPLIT = 8
+SLOT = 4
+PARTS = 8
 
 
 score_scale = 0.07216878364870322
@@ -11,11 +17,339 @@
 norm_eps = 1e-06
 
 
-def scatter_sum(partial):
-    devices = lax.axis_size("ep")
-    blocks = partial.astype(jnp.bfloat16).reshape(devices, -1, partial.shape[1])
-    arrived = lax.all_to_all(blocks, "ep", split_axis=0, concat_axis=0, tiled=True)
-    return jnp.sum(arrived.astype(jnp.float32), axis=0)
+def place(n):
+    me = lax.axis_index("ep")
+    core, side, outer = me % 2, (me // 2) % 2, me // 4
+    return me, core, side, outer, core * (n // 2) + side * (n // 4) + outer
+
+
+def greet(partners):
+    barrier = pltpu.get_barrier_semaphore()
+    for other in partners:
+        pl.semaphore_signal(
+            barrier, inc=1, device_id={"ep": other}, device_id_type=pl.DeviceIdType.MESH
+        )
+    pl.semaphore_wait(barrier, len(partners))
+
+
+def send(src, dst, send_sem, recv_sem, other):
+    copy = pltpu.make_async_remote_copy(
+        src_ref=src,
+        dst_ref=dst,
+        send_sem=send_sem,
+        recv_sem=recv_sem,
+        device_id={"ep": other},
+        device_id_type=pl.DeviceIdType.MESH,
+    )
+    copy.start()
+    return copy
+
+
+def row_picker(n, quarter):
+    row = lax.broadcasted_iota(jnp.int32, (SLOT * n, 16 * n), 0)
+    col = lax.broadcasted_iota(jnp.int32, (SLOT * n, 16 * n), 1)
+    return (col == ((row >> 2) << 4) + (row & 3) + 4 * quarter).astype(jnp.bfloat16)
+
+
+def scatter_sum(n, product, out_ref, own, leave, first, leave2, second, block, third, sems):
+    me, core, side, outer, slot = place(n)
+    rows = SLOT * n
+    outers = n // 4
+    send1, recv1, send2, recv2, send3, recv3 = sems
+    copies1, copies2, copies3 = {}, {}, []
+    width = out_ref.shape[2]
+    sums = {}
+
+    def half(value):
+        return pl.ds(pl.multiple_of(value * (rows // 2), 16), rows // 2)
+
+    def quarter(value):
+        return pl.ds(pl.multiple_of(value * (rows // 4), 16), rows // 4)
+
+    def begin(part):
+        value = product(part)
+        own[part] = value
+        leave[part] = value.astype(jnp.bfloat16)
+        copies1[part] = send(
+            leave.at[part, half(1 - core)],
+            first.at[part],
+            send1.at[part],
+            recv1.at[part],
+            me + 1 - 2 * core,
+        )
+
+    def over_x(part):
+        copies1[part].wait_recv()
+        value = own[part, half(core)] + first[part].astype(jnp.float32)
+        own[part, half(core)] = value
+        leave2[part] = value.astype(jnp.bfloat16)
+        copies2[part] = send(
+            leave2.at[part, quarter(1 - side)],
+            second.at[part],
+            send2.at[part],
+            recv2.at[part],
+            me + 2 - 4 * side,
+        )
+
+    def over_rest(part):
+        copies2[part].wait_recv()
+        value = own[part, quarter(2 * core + side)] + second[part].astype(jnp.float32)
+        sums[part] = value.astype(jnp.bfloat16)
+        if part % 4 < 3:
+            return
+        group = part // 4
+        row = lax.broadcasted_iota(jnp.int32, (16 * outers, rows // 4), 0)
+        col = lax.broadcasted_iota(jnp.int32, (16 * outers, rows // 4), 1)
+        total = jnp.zeros((16 * outers, width), jnp.float32)
+        for j in range(4):
+            pick = (((row >> 2) & 3) == j) & (col == ((row >> 4) << 2) + (row & 3))
+            total = total + jnp.dot(
+                pick.astype(jnp.bfloat16), sums[group * 4 + j], preferred_element_type=jnp.float32
+            )
+        block[group] = total.astype(jnp.bfloat16).reshape(outers, 16, width)
+        for d in range(1, outers):
+            there = lax.rem(outer + d, outers)
+            copies3.append(
+                send(
+                    block.at[group, there],
+                    third.at[group, d - 1],
+                    send3.at[group, d - 1],
+                    recv3.at[group, d - 1],
+                    there * 4 + side * 2 + core,
+                )
+            )
+
+    for step in range(PARTS + 2):
+        if step < PARTS:
+            begin(step)
+        if 1 <= step <= PARTS:
+            over_x(step - 1)
+        if step >= 2:
+            over_rest(step - 2)
+    for group in range(2):
+        value = block[group, outer].astype(jnp.float32)
+        for d in range(1, outers):
+            copies3[group * (outers - 1) + d - 1].wait_recv()
+            value = value + third[group, d - 1].astype(jnp.float32)
+        out_ref[group] = value
+    for copy in [*copies1.values(), *copies2.values(), *copies3]:
+        copy.wait_send()
+
+
+def sum_scratch(n, width):
+    rows, outers = SLOT * n, n // 4
+    dma = pltpu.SemaphoreType.DMA
+    return [
+        pltpu.VMEM((PARTS, rows, width), jnp.float32),
+        pltpu.VMEM((PARTS, rows, width), jnp.bfloat16),
+        pltpu.VMEM((PARTS, rows // 2, width), jnp.bfloat16),
+        pltpu.VMEM((PARTS, rows // 2, width), jnp.bfloat16),
+        pltpu.VMEM((PARTS, rows // 4, width), jnp.bfloat16),
+        pltpu.VMEM((2, outers, 16, width), jnp.bfloat16),
+        pltpu.VMEM((2, outers - 1, 16, width), jnp.bfloat16),
+        dma((PARTS,)),
+        dma((PARTS,)),
+        dma((PARTS,)),
+        dma((PARTS,)),
+        dma((2, outers - 1)),
+        dma((2, outers - 1)),
+    ]
+
+
+def project_kernel(
+    n, heads_ref, weight_ref, out_ref, arrived, lhs, weight, send_sem, recv_sem, load_sem, *rest
+):
+    me, core, side, outer, slot = place(n)
+    width = out_ref.shape[2]
+    quarter = heads_ref.shape[2]
+    loads = []
+    for part in range(PARTS):
+        load = pltpu.make_async_copy(
+            weight_ref.at[:, pl.ds(part * width, width)], weight.at[part], load_sem.at[part]
+        )
+        load.start()
+        loads.append(load)
+    greet([lax.rem(me + d, n) for d in range(1, n)])
+    copies = []
+    for d in range(1, n):
+        other = lax.rem(me + d, n)
+        copies.append(
+            send(
+                heads_ref.at[other],
+                arrived.at[slot],
+                send_sem.at[d - 1],
+                recv_sem.at[d - 1],
+                other,
+            )
+        )
+    arrived[slot] = heads_ref[me]
+    for copy in copies:
+        copy.wait_recv()
+    rows = arrived[...].reshape(16 * n, quarter)
+    for q in range(4):
+        lhs[q] = jnp.dot(row_picker(n, q), rows, preferred_element_type=jnp.float32).astype(
+            jnp.bfloat16
+        )
+
+    def product(part):
+        loads[part].wait()
+        total = jnp.zeros((SLOT * n, width), jnp.float32)
+        for q in range(4):
+            total = total + jnp.dot(
+                lhs[q],
+                weight[part, pl.ds(q * quarter, quarter)],
+                preferred_element_type=jnp.float32,
+            )
+        return total
+
+    scatter_sum(n, product, out_ref, *rest[:7], rest[7:])
+    for copy in copies:
+        copy.wait_send()
+
+
+def expert_kernel(
+    n, normed_ref, coeff_ref, gate_ref, up_ref, down_ref, out_ref,
+    gathered, gate, up, down, load_sem, send_a, recv_a, send_b, recv_b, send_c, recv_c, *rest
+):
+    me, core, side, outer, slot = place(n)
+    width = out_ref.shape[2]
+    outers = n // 4
+    quarter = normed_ref.shape[1]
+    loads = []
+    for i, (src, dst) in enumerate(((gate_ref, gate), (up_ref, up), (down_ref, down))):
+        load = pltpu.make_async_copy(src, dst, load_sem.at[i])
+        load.start()
+        loads.append(load)
+    across, sibling = me + 2 - 4 * side, me + 1 - 2 * core
+    peers = [lax.rem(outer + d, outers) * 4 + side * 2 + core for d in range(1, outers)]
+    greet([*peers, across, sibling])
+    gathered[slot] = normed_ref[...]
+    along = []
+    for d in range(1, outers):
+        along.append(
+            send(normed_ref, gathered.at[slot], send_a.at[d - 1], recv_a.at[d - 1], peers[d - 1])
+        )
+    over, core_copies = [], []
+    for d in range(outers):
+        if d:
+            along[d - 1].wait_recv()
+        index = core * (n // 2) + side * (n // 4) + lax.rem(outer - d + outers, outers)
+        held = gathered.at[index]
+        over.append(send(held, held, send_b.at[d], recv_b.at[d], across))
+        core_copies.append(send(held, held, send_c.at[d], recv_c.at[d], sibling))
+    for d in range(outers):
+        over[d].wait_recv()
+        index = core * (n // 2) + (1 - side) * (n // 4) + lax.rem(outer - d + outers, outers)
+        held = gathered.at[index]
+        core_copies.append(
+            send(held, held, send_c.at[outers + d], recv_c.at[outers + d], sibling)
+        )
+    for copy in core_copies:
+        copy.wait_recv()
+    loads[0].wait()
+    loads[1].wait()
+    rows = gathered[...].reshape(16 * n, quarter)
+    gate_val = jnp.zeros((SLOT * n, gate.shape[1]), jnp.float32)
+    up_val = jnp.zeros((SLOT * n, gate.shape[1]), jnp.float32)
+    for q in range(4):
+        lhs = jnp.dot(row_picker(n, q), rows, preferred_element_type=jnp.float32).astype(
+            jnp.bfloat16
+        )
+        span = pl.ds(q * quarter, quarter)
+        gate_val = gate_val + jnp.dot(lhs, gate[span], preferred_element_type=jnp.float32)
+        up_val = up_val + jnp.dot(lhs, up[span], preferred_element_type=jnp.float32)
+    active = (gate_val / (1.0 + jnp.exp(-gate_val)) * up_val).astype(jnp.bfloat16)
+    coeff = coeff_ref[...]
+    loads[2].wait()
+
+    def product(part):
+        value = jnp.dot(
+            active, down[:, pl.ds(part * width, width)], preferred_element_type=jnp.float32
+        )
+        return jnp.where(coeff != 0.0, value * coeff, 0.0)
+
+    scatter_sum(n, product, out_ref, *rest[:7], rest[7:])
+    for copy in [*along, *over, *core_copies]:
+        copy.wait_send()
+
+
+def slot_order(value, n):
+    rest = value.shape[1:]
+    return value.reshape(n // 4, 2, 2, *rest).swapaxes(0, 2).reshape(n, *rest)
+
+
+def unfold(summed, seq_count):
+    width = summed.shape[2]
+    split = summed.reshape(2, 4, SLOT, width).transpose(2, 0, 1, 3)
+    return split.reshape(SLOT, PARTS * width)[:seq_count]
+
+
+def project(flat_heads, weight):
+    n = lax.axis_size("ep")
+    depth, model_width = weight.shape
+    seq_count = flat_heads.shape[0]
+    quarter, width = depth // 4, model_width // PARTS
+    padded = jnp.pad(flat_heads, ((0, SLOT - seq_count), (0, 0)))
+    blocks = padded.reshape(SLOT, n, 4, quarter).transpose(1, 2, 0, 3).reshape(n, 16, quarter)
+    vmem = pl.BlockSpec(memory_space=pltpu.VMEM)
+    dma = pltpu.SemaphoreType.DMA
+    summed = pl.pallas_call(
+        functools.partial(project_kernel, n),
+        out_shape=jax.ShapeDtypeStruct((2, 16, width), jnp.float32),
+        in_specs=[vmem, pl.BlockSpec(memory_space=pl.ANY)],
+        out_specs=vmem,
+        scratch_shapes=[
+            pltpu.VMEM((n, 16, quarter), jnp.bfloat16),
+            pltpu.VMEM((4, SLOT * n, quarter), jnp.bfloat16),
+            pltpu.VMEM((PARTS, depth, width), jnp.bfloat16),
+            dma((n - 1,)),
+            dma((n - 1,)),
+            dma((PARTS,)),
+            *sum_scratch(n, width),
+        ],
+        compiler_params=pltpu.CompilerParams(
+            collective_id=0, has_side_effects=True, vmem_limit_bytes=56 * 2**20
+        ),
+    )(blocks, weight)
+    return unfold(summed, seq_count)
+
+
+def experts(normed, coeff, w_gate, w_up, w_down):
+    n = lax.axis_size("ep")
+    seq_count, model_width = normed.shape
+    hidden_width = w_gate.shape[1]
+    quarter, width = model_width // 4, model_width // PARTS
+    outers = n // 4
+    padded = jnp.pad(normed, ((0, SLOT - seq_count), (0, 0)))
+    block = padded.reshape(SLOT, 4, quarter).transpose(1, 0, 2).reshape(16, quarter)
+    weights = jnp.pad(slot_order(coeff, n), ((0, 0), (0, SLOT - seq_count)))
+    vmem = pl.BlockSpec(memory_space=pltpu.VMEM)
+    hbm = pl.BlockSpec(memory_space=pl.ANY)
+    dma = pltpu.SemaphoreType.DMA
+    summed = pl.pallas_call(
+        functools.partial(expert_kernel, n),
+        out_shape=jax.ShapeDtypeStruct((2, 16, width), jnp.float32),
+        in_specs=[vmem, vmem, hbm, hbm, hbm],
+        out_specs=vmem,
+        scratch_shapes=[
+            pltpu.VMEM((n, 16, quarter), jnp.bfloat16),
+            pltpu.VMEM((model_width, hidden_width), jnp.bfloat16),
+            pltpu.VMEM((model_width, hidden_width), jnp.bfloat16),
+            pltpu.VMEM((hidden_width, model_width), jnp.bfloat16),
+            dma((3,)),
+            dma((outers - 1,)),
+            dma((outers - 1,)),
+            dma((outers,)),
+            dma((outers,)),
+            dma((2 * outers,)),
+            dma((2 * outers,)),
+            *sum_scratch(n, width),
+        ],
+        compiler_params=pltpu.CompilerParams(
+            collective_id=1, has_side_effects=True, vmem_limit_bytes=56 * 2**20
+        ),
+    )(block, weights.reshape(SLOT * n, 1), w_gate, w_up, w_down)
+    return unfold(summed, seq_count)
 
 
 def local(
@@ -44,8 +378,7 @@
     spread = lax.all_to_all(
         jnp.repeat(spread.T, SPLIT, axis=0), "ep", split_axis=0, concat_axis=0, tiled=True
     )
-    coeff = spread.reshape(-1)
-    chosen = coeff != 0.0
+    coeff = spread.reshape(devices, seq_count)
     scores = jnp.einsum("thc,tlc->thl", q_latent, cache_latent, preferred_element_type=jnp.float32)
     scores = (
         scores + jnp.einsum("thr,tlr->thl", q_rope, cache_rope, preferred_element_type=jnp.float32)
@@ -60,19 +393,12 @@
         "thl,tlc->thc", attention_weight, cache_latent, preferred_element_type=jnp.float32
     ).astype(jnp.bfloat16)
     flat_heads = heads_out.reshape(seq_count, -1)
-    incoming = lax.all_to_all(flat_heads, "ep", split_axis=1, concat_axis=0, tiled=True)
-    row_block = incoming
-    attention = scatter_sum(jnp.dot(row_block, proj_weight, preferred_element_type=jnp.float32))
+    attention = project(flat_heads, proj_weight)
     hidden = resid.astype(jnp.float32) + attention
     normed = (
         hidden * lax.rsqrt(jnp.mean(hidden * hidden, axis=1, keepdims=True) + norm_eps) * norm_gain
     ).astype(jnp.bfloat16)
-    row_block = lax.all_gather(normed, "ep", axis=0, tiled=True)
-    gate_val = jnp.dot(row_block, w_gate[0], preferred_element_type=jnp.float32)
-    up_val = jnp.dot(row_block, w_up[0], preferred_element_type=jnp.float32)
-    active = (jax.nn.silu(gate_val) * up_val).astype(jnp.bfloat16)
-    partial_value = jnp.dot(active, w_down[0], preferred_element_type=jnp.float32)
-    mixture = scatter_sum(jnp.where(chosen[:, None], partial_value * coeff[:, None], 0.0))
+    mixture = experts(normed, coeff, w_gate[0], w_up[0], w_down[0])
     return (hidden + mixture).astype(jnp.bfloat16)
 
 

time: 129 us -> 89.6 us (0.69)
  Pallas kernels: 0 us -> 70.6 us
  blocking collectives: 49.7 us -> 0 us
  waiting for transfers between devices: 29 us -> 0.01 us
  matrix products: 21.7 us -> 2.32 us
  starting transfers between devices: 16.9 us -> 7.36 us
    pallas_call x0 -> x2, Pallas kernels: none -> 70.6 us  [the longest x1 35.6 us: experts(): pl.pallas_call(functools.partial(expert_kernel, n), out_shape=jax.ShapeDt...]
    all_to_all x2 -> x0, waiting for transfers between devices: 29 us -> none  [the longest x1 19 us: scatter_sum(): lax.all_to_all(blocks, 'ep', split_axis=0, concat_axis=0, tiled=True)]
    all_to_all x1 -> x0, blocking collectives: 25.3 us -> none  [scatter_sum(): lax.all_to_all(blocks, 'ep', split_axis=0, concat_axis=0, tiled=True)]
    all_gather x1 -> x0, blocking collectives: 24.5 us -> none  [local(): row_block = lax.all_gather(normed, 'ep', axis=0, tiled=True)]
    dot_general x4 -> x0, matrix products: 17.2 us -> none  [the longest x1 12.1 us: local(): jnp.dot(row_block, proj_weight, preferred_element_type=jnp.float32)]
    all_to_all x2 -> x0, starting transfers between devices: 13.5 us -> none  [the longest x1 7.35 us: local(): lax.all_to_all(flat_heads, 'ep', split_axis=1, concat_axis=0, tiled=True)]
    all_to_all x1, starting transfers between devices: 3.47 us -> 7.36 us  [local(): lax.all_to_all(jnp.repeat(spread.T, SPLIT, axis=0), 'ep', split_axis=0, c...]
    all_to_all x4 -> x0, local copies, waits for them, and re-layouts: 2.6 us -> none  [the longest x3 2.08 us: local(): lax.all_to_all(flat_heads, 'ep', split_axis=1, concat_axis=0, tiled=True)]
  transfers between devices with their start and end apart: 3 -> 1, of which waited for: 2 -> 0; matrix products, arithmetic and copies ran while one was open for 12% -> 7% of each run, Pallas kernels for 0% -> 39%
where the time goes in v2:
time: 89.6 us; the launch traced here: 89.2 us
  Pallas kernels  70.6 us (79%)
  starting transfers between devices  7.36 us (8%)
  local copies, waits for them, and re-layouts  4.88 us (5%)
  other arithmetic  3.89 us (4%)
  matrix products  2.32 us (3%)
    pallas_call x1, Pallas kernels, experts(): pl.pallas_call(functools.partial(expert_kernel, n), out_shape=jax.ShapeDt...  35.6 us
    pallas_call x1, Pallas kernels, project(): pl.pallas_call(functools.partial(project_kernel, n), out_shape=jax.ShapeD...  35.1 us
    all_to_all x1, starting transfers between devices, local(): lax.all_to_all(jnp.repeat(spread.T, SPLIT, axis=0), 'ep', split_axis=0, c...  7.36 us
    reshape x2, local copies, waits for them, and re-layouts, unfold(): split = summed.reshape(2, 4, SLOT, width).transpose(2, 0, 1, 3)  1.86 us
  transfers between devices with their start and end apart: 1, of which 0 were waited for; matrix products, arithmetic and copies ran while one was open for 7% of the time, Pallas kernels for 39%

profile of v2, /device:TPU:0, one launch (start us, length us, event | category | flops | bytes accessed | tf_op | source)
XLA Modules:
  0.0 89.2 jit_solution(928310943476314971)
XLA Ops:
  0.0 0.0 copy-start
  0.0 0.0 copy-start.4
  0.0 0.0 copy-start.3
  0.0 0.8 reduce_sum.38
  0.8 0.7 multiply_divide_fusion
  1.5 0.7 fusion.8
  2.2 0.6 broadcast_in_dim.48.clone
  2.8 7.4 %all-to-all-start = ((f32[16,1,3]{2,1,0:T(1,128)}), f32[16,1,3]{2,1,0:T(1,128)S(1)}, u32[]{:S(2)}, u32[]{:S(2)}) async-start(f32[16,1,3]{2,1,0:T(1,128)} %bitcast.7), calls=%async_computation | async-start | bytes 16384 | tf_op jit(solution)/shard_map/all_to_all | solution.py:378
  10.2 0.7 iota_compare_fusion
  10.9 0.0 copy-done
  10.9 1.5 %fusion.10 = f32[3,64,512]{2,1,0:T(8,128)S(1)} fusion(bf16[3,64,512]{2,1,0:T(8,128)(2,1)} %param.14, bf16[3,512,512]{2,1,0:T(8,128)(2,1)S(1)} %copy-done), kind=kOutput, calls=%fused_computation.21 | convolution fusion | flops 100663296 | bytes 2162688 | tf_op jit(solution)/shard_map/thc,tlc->thl/dot_general | solution.py:382
  12.4 0.0 copy-done.4
  12.4 0.0 copy-done.3
  12.4 0.4 fusion.9
  12.8 0.4 fusion.6
  13.3 0.2 copy.56
  13.4 0.1 pad.12
  13.6 0.8 reshape.76.heads_ref
  14.3 0.0 copy-start.1
  14.3 0.0 copy-start.2
  14.3 35.1 %shard_map.127 = f32[2,16,896]{2,1,0:T(8,128)} custom-call(bf16[16,16,512]{2,1,0:T(8,128)(2,1)} %reshape.76.heads_ref, bf16[2048,7168]{1,0:T(8,128)(2,1)} %weight_ref.1), custom_call_target="tpu_custom_call" | custom-call | tf_op jit(solution)/shard_map/pallas_call | solution.py:296
  49.4 0.9 %reshape.77 = f32[2,4,4,896]{3,2,1,0:T(4,128)S(1)} reshape(f32[2,16,896]{2,1,0:T(8,128)} %shard_map.127) | data formatting | bytes 229376 | tf_op jit(solution)/shard_map/reshape | solution.py:283
  50.3 0.0 copy-done.1
  50.4 0.2 multiply_reduce_fusion
  50.5 0.0 copy-done.2
  50.6 0.1 multiply_convert_fusion
  50.7 0.6 reshape.79.normed_ref
  51.3 0.0 all-to-all-done
  51.3 0.7 reshape.84.coeff_ref
  52.0 35.6 %shard_map.128 = f32[2,16,896]{2,1,0:T(8,128)} custom-call(bf16[16,1792]{1,0:T(8,128)(2,1)} %reshape.79.normed_ref, f32[64,1]{1,0:T(8,128)} %reshape.84.coeff_ref, bf16[7168,128]{1,0:T(8,128)(2,1)} %bitcast.30, bf16[7168,128]{1,0:T(8,128)(2,1)} %bitcast.31, bf16[128,7168]{1,0:T(8,128)(2,1)} %bitcast.32), custom_call_target="tpu_custom_call" | custom-call | tf_op jit(solution)/shard_map/pallas_call | solution.py:329
  87.6 0.9 %reshape.83 = f32[2,4,4,896]{3,2,1,0:T(4,128)S(1)} reshape(f32[2,16,896]{2,1,0:T(8,128)} %shard_map.128) | data formatting | bytes 229376 | tf_op jit(solution)/shard_map/reshape | solution.py:283
  88.5 0.7 add_convert_fusion
  (4 shorter events, 0.0 us)
Async XLA Ops:
  0.0 10.9 %copy-start = (bf16[3,512,512]{2,1,0:T(8,128)(2,1)S(1)}, bf16[3,512,512]{2,1,0:T(8,128)(2,1)}, u32[]{:S(2)}) copy-start(bf16[3,512,512]{2,1,0:T(8,128)(2,1)} %param.16) | copy-start | bytes 4718596
  0.0 12.4 %copy-start.4 = (bf16[3,64,64]{2,1,0:T(8,128)(2,1)S(1)}, bf16[3,64,64]{2,1,0:T(8,128)(2,1)}, u32[]{:S(2)}) copy-start(bf16[3,64,64]{2,1,0:T(8,128)(2,1)} %param.15) | copy-start | bytes 73732
  0.0 12.4 %copy-start.3 = (bf16[3,512,64]{1,2,0:T(8,128)(2,1)S(1)}, bf16[3,512,64]{1,2,0:T(8,128)(2,1)}, u32[]{:S(2)}) copy-start(bf16[3,512,64]{1,2,0:T(8,128)(2,1)} %param.17) | copy-start | bytes 589828
  2.8 48.5 %all-to-all-start = ((f32[16,1,3]{2,1,0:T(1,128)}), f32[16,1,3]{2,1,0:T(1,128)S(1)}, u32[]{:S(2)}, u32[]{:S(2)}) async-start(f32[16,1,3]{2,1,0:T(1,128)} %bitcast.7), calls=%async_computation | async-start | bytes 16384 | tf_op jit(solution)/shard_map/all_to_all | solution.py:378
  14.3 36.0 %copy-start.1 = (bf16[3,7168]{1,0:T(4,128)(2,1)S(1)}, bf16[3,7168]{1,0:T(4,128)(2,1)}, u32[]{:S(2)}) copy-start(bf16[3,7168]{1,0:T(4,128)(2,1)} %param.13) | copy-start | bytes 129028
  14.3 36.2 %copy-start.2 = (f32[7168]{0:T(1024)S(1)}, f32[7168]{0:T(1024)}, u32[]{:S(2)}) copy-start(f32[7168]{0:T(1024)} %param.20) | copy-start | bytes 86020

commit v3 on v2

--- a/solution.py
+++ b/solution.py
@@ -9,6 +9,7 @@
 
 SPLIT = 8
 SLOT = 4
+LANES = 128
 PARTS = 8
 
 
@@ -51,13 +52,13 @@
     return (col == ((row >> 2) << 4) + (row & 3) + 4 * quarter).astype(jnp.bfloat16)
 
 
-def scatter_sum(n, product, out_ref, own, leave, first, leave2, second, block, third, sems):
+def scatter_sum(n, product, finish, lags, own, leave, first, leave2, second, block, third, sems):
     me, core, side, outer, slot = place(n)
     rows = SLOT * n
     outers = n // 4
     send1, recv1, send2, recv2, send3, recv3 = sems
     copies1, copies2, copies3 = {}, {}, []
-    width = out_ref.shape[2]
+    width = own.shape[2]
     sums = {}
 
     def half(value):
@@ -119,19 +120,19 @@
                 )
             )
 
-    for step in range(PARTS + 2):
+    for step in range(PARTS + lags[1]):
         if step < PARTS:
             begin(step)
-        if 1 <= step <= PARTS:
-            over_x(step - 1)
-        if step >= 2:
-            over_rest(step - 2)
+        if 0 <= step - lags[0] < PARTS:
+            over_x(step - lags[0])
+        if step >= lags[1]:
+            over_rest(step - lags[1])
     for group in range(2):
         value = block[group, outer].astype(jnp.float32)
         for d in range(1, outers):
             copies3[group * (outers - 1) + d - 1].wait_recv()
             value = value + third[group, d - 1].astype(jnp.float32)
-        out_ref[group] = value
+        finish(group, value)
     for copy in [*copies1.values(), *copies2.values(), *copies3]:
         copy.wait_send()
 
@@ -202,19 +203,21 @@
             )
         return total
 
-    scatter_sum(n, product, out_ref, *rest[:7], rest[7:])
+    def finish(group, value):
+        out_ref[group] = value
+
+    scatter_sum(n, product, finish, (2, 4), *rest[:7], rest[7:])
     for copy in copies:
         copy.wait_send()
 
 
 def expert_kernel(
-    n, normed_ref, coeff_ref, gate_ref, up_ref, down_ref, out_ref,
-    gathered, gate, up, down, load_sem, send_a, recv_a, send_b, recv_b, send_c, recv_c, *rest
+    n, summed_ref, resid_ref, gain_ref, tag_ref, gate_ref, up_ref, down_ref, out_ref,
+    hidden, gathered, gate, up, down, load_sem, send_a, recv_a, send_b, recv_b, send_c, recv_c, *rest
 ):
     me, core, side, outer, slot = place(n)
     width = out_ref.shape[2]
     outers = n // 4
-    quarter = normed_ref.shape[1]
     loads = []
     for i, (src, dst) in enumerate(((gate_ref, gate), (up_ref, up), (down_ref, down))):
         load = pltpu.make_async_copy(src, dst, load_sem.at[i])
@@ -223,11 +226,22 @@
     across, sibling = me + 2 - 4 * side, me + 1 - 2 * core
     peers = [lax.rem(outer + d, outers) * 4 + side * 2 + core for d in range(1, outers)]
     greet([*peers, across, sibling])
-    gathered[slot] = normed_ref[...]
+    squares = jnp.zeros((16, 1), jnp.float32)
+    for group in range(2):
+        value = summed_ref[group] + resid_ref[group]
+        hidden[group] = value
+        squares = squares + jnp.sum(value * value, axis=1, keepdims=True)
+    total = squares[0:4] + squares[4:8] + squares[8:12] + squares[12:16]
+    scale = lax.rsqrt(total / (PARTS * width) + norm_eps)
+    scale = jnp.concatenate([scale] * 4, axis=0)
+    for group in range(2):
+        normed = (hidden[group] * scale * gain_ref[group]).astype(jnp.bfloat16)
+        gathered[slot, group] = normed + tag_ref[group]
+    mine = gathered.at[slot]
     along = []
     for d in range(1, outers):
         along.append(
-            send(normed_ref, gathered.at[slot], send_a.at[d - 1], recv_a.at[d - 1], peers[d - 1])
+            send(mine, mine, send_a.at[d - 1], recv_a.at[d - 1], peers[d - 1])
         )
     over, core_copies = [], []
     for d in range(outers):
@@ -248,18 +262,28 @@
         copy.wait_recv()
     loads[0].wait()
     loads[1].wait()
-    rows = gathered[...].reshape(16 * n, quarter)
     gate_val = jnp.zeros((SLOT * n, gate.shape[1]), jnp.float32)
     up_val = jnp.zeros((SLOT * n, gate.shape[1]), jnp.float32)
-    for q in range(4):
-        lhs = jnp.dot(row_picker(n, q), rows, preferred_element_type=jnp.float32).astype(
-            jnp.bfloat16
-        )
-        span = pl.ds(q * quarter, quarter)
+    for part in range(PARTS):
+        rows = gathered[:, part // 4].reshape(16 * n, width)
+        lhs = jnp.dot(
+            row_picker(n, part % 4), rows, preferred_element_type=jnp.float32
+        ).astype(jnp.bfloat16)
+        span = pl.ds(part * width, width)
         gate_val = gate_val + jnp.dot(lhs, gate[span], preferred_element_type=jnp.float32)
         up_val = up_val + jnp.dot(lhs, up[span], preferred_element_type=jnp.float32)
+    row = lax.broadcasted_iota(jnp.int32, (SLOT * n, 16 * n), 0)
+    col = lax.broadcasted_iota(jnp.int32, (SLOT * n, 16 * n), 1)
+    tags = jnp.dot(
+        (col == ((row >> 2) << 4) + 3).astype(jnp.bfloat16),
+        gathered[:, 0].reshape(16 * n, width)[:, : 2 * LANES],
+        preferred_element_type=jnp.float32,
+    )
+    row = lax.broadcasted_iota(jnp.int32, (SLOT * n, 2 * LANES), 0)
+    col = lax.broadcasted_iota(jnp.int32, (SLOT * n, 2 * LANES), 1)
+    wanted = (col & (LANES - 1)) == (me // SPLIT) * SLOT + (row & 3)
+    coeff = jnp.sum(jnp.where(wanted, tags, 0.0), axis=1, keepdims=True)
     active = (gate_val / (1.0 + jnp.exp(-gate_val)) * up_val).astype(jnp.bfloat16)
-    coeff = coeff_ref[...]
     loads[2].wait()
 
     def product(part):
@@ -268,14 +292,19 @@
         )
         return jnp.where(coeff != 0.0, value * coeff, 0.0)
 
-    scatter_sum(n, product, out_ref, *rest[:7], rest[7:])
+    def finish(group, value):
+        out_ref[group] = (hidden[group] + value).astype(jnp.bfloat16)
+
+    scatter_sum(n, product, finish, (PARTS, 2 * PARTS), *rest[:7], rest[7:])
     for copy in [*along, *over, *core_copies]:
         copy.wait_send()
 
 
-def slot_order(value, n):
-    rest = value.shape[1:]
-    return value.reshape(n // 4, 2, 2, *rest).swapaxes(0, 2).reshape(n, *rest)
+def fold(value):
+    seq_count, model_width = value.shape
+    width = model_width // PARTS
+    padded = jnp.pad(value, ((0, SLOT - seq_count), (0, 0)))
+    return padded.reshape(SLOT, 2, 4, width).transpose(1, 2, 0, 3).reshape(2, 16, width)
 
 
 def unfold(summed, seq_count):
@@ -311,28 +340,32 @@
             collective_id=0, has_side_effects=True, vmem_limit_bytes=56 * 2**20
         ),
     )(blocks, weight)
-    return unfold(summed, seq_count)
-
-
-def experts(normed, coeff, w_gate, w_up, w_down):
+    return summed
+
+
+def experts(summed, resid, norm_gain, spread, w_gate, w_up, w_down):
     n = lax.axis_size("ep")
-    seq_count, model_width = normed.shape
+    seq_count, model_width = resid.shape
     hidden_width = w_gate.shape[1]
-    quarter, width = model_width // 4, model_width // PARTS
+    width = model_width // PARTS
     outers = n // 4
-    padded = jnp.pad(normed, ((0, SLOT - seq_count), (0, 0)))
-    block = padded.reshape(SLOT, 4, quarter).transpose(1, 0, 2).reshape(16, quarter)
-    weights = jnp.pad(slot_order(coeff, n), ((0, 0), (0, SLOT - seq_count)))
+    gain = jnp.repeat(norm_gain.reshape(2, 4, width), SLOT, axis=1)
+    weights = jnp.pad(spread.T, ((0, 0), (0, SLOT - seq_count))).reshape(-1)
+    weights = jnp.pad(weights, (0, LANES - weights.shape[0]))
+    high = lax.reduce_precision(weights, 8, 7)
+    tag_row = jnp.concatenate([high, weights - high]).astype(jnp.bfloat16)
+    tags = jnp.pad(tag_row[None, None, :], ((0, 1), (3, 12), (0, width - 2 * LANES)))
     vmem = pl.BlockSpec(memory_space=pltpu.VMEM)
     hbm = pl.BlockSpec(memory_space=pl.ANY)
     dma = pltpu.SemaphoreType.DMA
-    summed = pl.pallas_call(
+    mixed = pl.pallas_call(
         functools.partial(expert_kernel, n),
-        out_shape=jax.ShapeDtypeStruct((2, 16, width), jnp.float32),
-        in_specs=[vmem, vmem, hbm, hbm, hbm],
+        out_shape=jax.ShapeDtypeStruct((2, 16, width), jnp.bfloat16),
+        in_specs=[vmem, vmem, vmem, vmem, hbm, hbm, hbm],
         out_specs=vmem,
         scratch_shapes=[
-            pltpu.VMEM((n, 16, quarter), jnp.bfloat16),
+            pltpu.VMEM((2, 16, width), jnp.float32),
+            pltpu.VMEM((n, 2, 16, width), jnp.bfloat16),
             pltpu.VMEM((model_width, hidden_width), jnp.bfloat16),
             pltpu.VMEM((model_width, hidden_width), jnp.bfloat16),
             pltpu.VMEM((hidden_width, model_width), jnp.bfloat16),
@@ -348,8 +381,8 @@
         compiler_params=pltpu.CompilerParams(
             collective_id=1, has_side_effects=True, vmem_limit_bytes=56 * 2**20
         ),
-    )(block, weights.reshape(SLOT * n, 1), w_gate, w_up, w_down)
-    return unfold(summed, seq_count)
+    )(summed, fold(resid.astype(jnp.float32)), gain, tags, w_gate, w_up, w_down)
+    return unfold(mixed, seq_count)
 
 
 def local(
@@ -375,10 +408,6 @@
     expert_cols = jnp.arange(experts_all, dtype=jnp.int32)
     named = expert_ids[:, :, None] == expert_cols
     spread = jnp.sum(jnp.where(named, route_weight[:, :, None], 0.0), axis=1)
-    spread = lax.all_to_all(
-        jnp.repeat(spread.T, SPLIT, axis=0), "ep", split_axis=0, concat_axis=0, tiled=True
-    )
-    coeff = spread.reshape(devices, seq_count)
     scores = jnp.einsum("thc,tlc->thl", q_latent, cache_latent, preferred_element_type=jnp.float32)
     scores = (
         scores + jnp.einsum("thr,tlr->thl", q_rope, cache_rope, preferred_element_type=jnp.float32)
@@ -393,13 +422,8 @@
         "thl,tlc->thc", attention_weight, cache_latent, preferred_element_type=jnp.float32
     ).astype(jnp.bfloat16)
     flat_heads = heads_out.reshape(seq_count, -1)
-    attention = project(flat_heads, proj_weight)
-    hidden = resid.astype(jnp.float32) + attention
-    normed = (
-        hidden * lax.rsqrt(jnp.mean(hidden * hidden, axis=1, keepdims=True) + norm_eps) * norm_gain
-    ).astype(jnp.bfloat16)
-    mixture = experts(normed, coeff, w_gate[0], w_up[0], w_down[0])
-    return (hidden + mixture).astype(jnp.bfloat16)
+    summed = project(flat_heads, proj_weight)
+    return experts(summed, resid, norm_gain, spread, w_gate[0], w_up[0], w_down[0])
 
 
 def solution(mesh):

time: 89.6 us -> 72.1 us (0.80)
  Pallas kernels: 70.6 us -> 63.2 us
  starting transfers between devices: 7.36 us -> 0 us
  other arithmetic: 3.89 us -> 0.77 us
    all_to_all x1 -> x0, starting transfers between devices: 7.36 us -> none  [local(): lax.all_to_all(jnp.repeat(spread.T, SPLIT, axis=0), 'ep', split_axis=0, c...]
    pallas_call x1, Pallas kernels: 35.6 us -> 29.7 us  [experts(): pl.pallas_call(functools.partial(expert_kernel, n), out_shape=jax.ShapeDt...]
    pallas_call x1, Pallas kernels: 35.1 us -> 33.5 us  [project(): pl.pallas_call(functools.partial(project_kernel, n), out_shape=jax.ShapeD...]
    unnamed x12 -> x17, local copies, waits for them, and re-layouts: 0.19 us -> 1.6 us
    reshape x2 -> x1, local copies, waits for them, and re-layouts: 1.86 us -> 1.46 us  [unfold(): split = summed.reshape(2, 4, SLOT, width).transpose(2, 0, 1, 3)]
  transfers between devices with their start and end apart: 1 -> 0, of which waited for: 0 -> 0; matrix products, arithmetic and copies ran while one was open for 7% -> 0% of each run, Pallas kernels for 39% -> 0%
where the time goes in v3:
time: 72.1 us; the launch traced here: 71.9 us
  Pallas kernels  63.2 us (88%)
  local copies, waits for them, and re-layouts  5.44 us (8%)
  matrix products  2.32 us (3%)
  other arithmetic  0.77 us (1%)
    pallas_call x1, Pallas kernels, project(): pl.pallas_call(functools.partial(project_kernel, n), out_shape=jax.ShapeD...  33.5 us
    pallas_call x1, Pallas kernels, experts(): pl.pallas_call(functools.partial(expert_kernel, n), out_shape=jax.ShapeDt...  29.7 us
    unnamed x17, local copies, waits for them, and re-layouts  1.6 us
    dot_general x1, matrix products, local(): jnp.einsum('thc,tlc->thl', q_latent, cache_latent, preferred_element_type...  1.51 us
    reshape x1, local copies, waits for them, and re-layouts, unfold(): split = summed.reshape(2, 4, SLOT, width).transpose(2, 0, 1, 3)  1.46 us

profile of v3, /device:TPU:0, one launch (start us, length us, event | category | flops | bytes accessed | tf_op | source)
XLA Modules:
  0.0 71.9 jit_solution(8552344391283019236)
XLA Ops:
  0.0 0.0 copy-start
  0.0 0.0 copy-start.5
  0.0 0.0 copy-start.7
  0.0 0.0 copy-start.6
  0.0 1.4 %copy-done = bf16[3,512,512]{2,1,0:T(8,128)(2,1)S(1)} copy-done((bf16[3,512,512]{2,1,0:T(8,128)(2,1)S(1)}, bf16[3,512,512]{2,1,0:T(8,128)(2,1)}, u32[]{:S(2)}) %copy-start) | copy-done | bytes 1572888
  1.4 1.5 %fusion.23 = f32[3,64,512]{2,1,0:T(8,128)S(1)} fusion(bf16[3,64,512]{2,1,0:T(8,128)(2,1)} %param.14, bf16[3,512,512]{2,1,0:T(8,128)(2,1)S(1)} %copy-done), kind=kOutput, calls=%fused_computation.36 | convolution fusion | flops 100663296 | bytes 2162688 | tf_op jit(solution)/shard_map/thc,tlc->thl/dot_general | solution.py:411
  2.9 0.0 copy-done.5
  2.9 0.1 iota_compare_fusion.4
  3.0 0.0 copy-done.7
  3.0 0.0 copy-done.6
  3.0 0.4 fusion.22
  3.4 0.4 fusion.6
  3.8 0.2 copy.20
  4.0 0.1 pad.21
  4.1 0.8 %reshape.91.heads_ref = bf16[16,16,512]{2,1,0:T(8,128)(2,1)} reshape(bf16[16,4,4,512]{3,2,1,0:T(4,128)(2,1)S(1)} %bitcast.30) | data formatting | bytes 524288 | tf_op jit(solution)/shard_map/reshape | solution.py:322
  4.9 0.0 copy-start.3
  4.9 0.0 copy-start.4
  4.9 0.0 copy-start.1
  4.9 0.0 copy-start.2
  4.9 33.5 %shard_map.127.summed_ref = f32[2,16,896]{2,1,0:T(8,128)} custom-call(bf16[16,16,512]{2,1,0:T(8,128)(2,1)} %reshape.91.heads_ref, bf16[2048,7168]{1,0:T(8,128)(2,1)} %weight_ref.1), custom_call_target="tpu_custom_call" | custom-call | tf_op jit(solution)/shard_map/pallas_call | solution.py:325
  38.4 0.0 copy-done.3
  38.5 0.0 copy-done.4
  38.5 0.1 reshape.97
  38.6 0.6 fusion.15.tag_ref
  39.3 0.0 copy-done.1
  39.3 0.7 reshape.100.resid_ref
  40.0 0.0 copy-done.2
  40.0 0.7 reshape.96.gain_ref
  40.7 29.7 %shard_map.128 = bf16[2,16,896]{2,1,0:T(8,128)(2,1)} custom-call(f32[2,16,896]{2,1,0:T(8,128)} %shard_map.127.summed_ref, f32[2,16,896]{2,1,0:T(8,128)} %reshape.100.resid_ref, f32[2,16,896]{2,1,0:T(8,128)} %reshape.96.gain_ref, bf16[2,16,896]{2,1,0:T(8,128)(2,1)} %fusion.15.tag_ref, bf16[7168,128]{1,0:T(8,128)(2,1)} %bitcast.26, ...), custom_call_target="tpu_custom_call" | custom-call | tf_op jit(solution)/shard_map/pallas_call | solution.py:361
  70.4 1.5 %reshape.98 = bf16[2,4,4,896]{3,2,1,0:T(4,128)(2,1)} reshape(bf16[2,16,896]{2,1,0:T(8,128)(2,1)} %shard_map.128) | data formatting | bytes 114688 | tf_op jit(solution)/shard_map/reshape | solution.py:312
  (9 shorter events, 0.1 us)
Async XLA Ops:
  0.0 1.4 %copy-start = (bf16[3,512,512]{2,1,0:T(8,128)(2,1)S(1)}, bf16[3,512,512]{2,1,0:T(8,128)(2,1)}, u32[]{:S(2)}) copy-start(bf16[3,512,512]{2,1,0:T(8,128)(2,1)} %param.16) | copy-start | bytes 4718596
  0.0 2.9 %copy-start.5 = (s32[3]{0:T(128)S(1)}, s32[3]{0:T(128)}, u32[]{:S(2)}) copy-start(s32[3]{0:T(128)} %param.18) | copy-start | bytes 40
  0.0 3.0 %copy-start.7 = (bf16[3,64,64]{2,1,0:T(8,128)(2,1)S(1)}, bf16[3,64,64]{2,1,0:T(8,128)(2,1)}, u32[]{:S(2)}) copy-start(bf16[3,64,64]{2,1,0:T(8,128)(2,1)} %param.15) | copy-start | bytes 73732
  0.0 3.0 %copy-start.6 = (bf16[3,512,64]{1,2,0:T(8,128)(2,1)S(1)}, bf16[3,512,64]{1,2,0:T(8,128)(2,1)}, u32[]{:S(2)}) copy-start(bf16[3,512,64]{1,2,0:T(8,128)(2,1)} %param.17) | copy-start | bytes 589828
  4.9 33.6 %copy-start.3 = (f32[3,2]{0,1:T(2,128)S(1)}, f32[3,2]{0,1:T(2,128)}, u32[]{:S(2)}) copy-start(f32[3,2]{0,1:T(2,128)} %param.22) | copy-start | bytes 76
  4.9 33.6 %copy-start.4 = (s32[3,2]{0,1:T(2,128)S(1)}, s32[3,2]{0,1:T(2,128)}, u32[]{:S(2)}) copy-start(s32[3,2]{0,1:T(2,128)} %param.21) | copy-start | bytes 76
  4.9 34.4 %copy-start.1 = (bf16[3,7168]{1,0:T(4,128)(2,1)S(1)}, bf16[3,7168]{1,0:T(4,128)(2,1)}, u32[]{:S(2)}) copy-start(bf16[3,7168]{1,0:T(4,128)(2,1)} %param.13) | copy-start | bytes 129028
  4.9 35.1 %copy-start.2 = (f32[7168]{0:T(1024)S(1)}, f32[7168]{0:T(1024)}, u32[]{:S(2)}) copy-start(f32[7168]{0:T(1024)} %param.20) | copy-start | bytes 86020

commit v4 on v3

--- a/solution.py
+++ b/solution.py
@@ -206,7 +206,7 @@
     def finish(group, value):
         out_ref[group] = value
 
-    scatter_sum(n, product, finish, (2, 4), *rest[:7], rest[7:])
+    scatter_sum(n, product, finish, (3, 6), *rest[:7], rest[7:])
     for copy in copies:
         copy.wait_send()
 

time: 72.1 us -> 70.5 us (0.978)
  Pallas kernels: 63.2 us -> 61.6 us
    pallas_call x1, Pallas kernels: 33.5 us -> 31.9 us  [project(): pl.pallas_call(functools.partial(project_kernel, n), out_shape=jax.ShapeD...]
where the time goes in v4:
time: 70.5 us; the launch traced here: 70.2 us
  Pallas kernels  61.6 us (87%)
  local copies, waits for them, and re-layouts  5.44 us (8%)
  matrix products  2.32 us (3%)
  other arithmetic  0.77 us (1%)
    pallas_call x1, Pallas kernels, project(): pl.pallas_call(functools.partial(project_kernel, n), out_shape=jax.ShapeD...  31.9 us
    pallas_call x1, Pallas kernels, experts(): pl.pallas_call(functools.partial(expert_kernel, n), out_shape=jax.ShapeDt...  29.7 us
    unnamed x17, local copies, waits for them, and re-layouts  1.6 us
    dot_general x1, matrix products, local(): jnp.einsum('thc,tlc->thl', q_latent, cache_latent, preferred_element_type...  1.51 us
    reshape x1, local copies, waits for them, and re-layouts, unfold(): split = summed.reshape(2, 4, SLOT, width).transpose(2, 0, 1, 3)  1.46 us

profile of v4, /device:TPU:0, one launch (start us, length us, event | category | flops | bytes accessed | tf_op | source)
XLA Modules:
  0.0 70.2 jit_solution(5839578863679168278)
XLA Ops:
  0.0 0.0 copy-start
  0.0 0.0 copy-start.5
  0.0 0.0 copy-start.7
  0.0 0.0 copy-start.6
  0.0 1.4 %copy-done = bf16[3,512,512]{2,1,0:T(8,128)(2,1)S(1)} copy-done((bf16[3,512,512]{2,1,0:T(8,128)(2,1)S(1)}, bf16[3,512,512]{2,1,0:T(8,128)(2,1)}, u32[]{:S(2)}) %copy-start) | copy-done | bytes 1572888
  1.4 1.5 %fusion.23 = f32[3,64,512]{2,1,0:T(8,128)S(1)} fusion(bf16[3,64,512]{2,1,0:T(8,128)(2,1)} %param.14, bf16[3,512,512]{2,1,0:T(8,128)(2,1)S(1)} %copy-done), kind=kOutput, calls=%fused_computation.36 | convolution fusion | flops 100663296 | bytes 2162688 | tf_op jit(solution)/shard_map/thc,tlc->thl/dot_general | solution.py:411
  2.9 0.0 copy-done.5
  2.9 0.1 iota_compare_fusion.4
  3.0 0.0 copy-done.7
  3.0 0.0 copy-done.6
  3.0 0.4 fusion.22
  3.4 0.4 fusion.6
  3.8 0.2 copy.20
  4.0 0.1 pad.21
  4.1 0.8 %reshape.91.heads_ref = bf16[16,16,512]{2,1,0:T(8,128)(2,1)} reshape(bf16[16,4,4,512]{3,2,1,0:T(4,128)(2,1)S(1)} %bitcast.30) | data formatting | bytes 524288 | tf_op jit(solution)/shard_map/reshape | solution.py:322
  4.9 0.0 copy-start.3
  4.9 0.0 copy-start.4
  4.9 0.0 copy-start.1
  4.9 0.0 copy-start.2
  4.9 31.9 %shard_map.127.summed_ref = f32[2,16,896]{2,1,0:T(8,128)} custom-call(bf16[16,16,512]{2,1,0:T(8,128)(2,1)} %reshape.91.heads_ref, bf16[2048,7168]{1,0:T(8,128)(2,1)} %weight_ref.1), custom_call_target="tpu_custom_call" | custom-call | tf_op jit(solution)/shard_map/pallas_call | solution.py:325
  36.8 0.0 copy-done.3
  36.8 0.0 copy-done.4
  36.9 0.1 reshape.97
  37.0 0.6 fusion.15.tag_ref
  37.6 0.0 copy-done.1
  37.6 0.7 reshape.100.resid_ref
  38.3 0.0 copy-done.2
  38.4 0.7 reshape.96.gain_ref
  39.0 29.7 %shard_map.128 = bf16[2,16,896]{2,1,0:T(8,128)(2,1)} custom-call(f32[2,16,896]{2,1,0:T(8,128)} %shard_map.127.summed_ref, f32[2,16,896]{2,1,0:T(8,128)} %reshape.100.resid_ref, f32[2,16,896]{2,1,0:T(8,128)} %reshape.96.gain_ref, bf16[2,16,896]{2,1,0:T(8,128)(2,1)} %fusion.15.tag_ref, bf16[7168,128]{1,0:T(8,128)(2,1)} %bitcast.26, ...), custom_call_target="tpu_custom_call" | custom-call | tf_op jit(solution)/shard_map/pallas_call | solution.py:361
  68.8 1.5 %reshape.98 = bf16[2,4,4,896]{3,2,1,0:T(4,128)(2,1)} reshape(bf16[2,16,896]{2,1,0:T(8,128)(2,1)} %shard_map.128) | data formatting | bytes 114688 | tf_op jit(solution)/shard_map/reshape | solution.py:312
  (9 shorter events, 0.1 us)
Async XLA Ops:
  0.0 1.4 %copy-start = (bf16[3,512,512]{2,1,0:T(8,128)(2,1)S(1)}, bf16[3,512,512]{2,1,0:T(8,128)(2,1)}, u32[]{:S(2)}) copy-start(bf16[3,512,512]{2,1,0:T(8,128)(2,1)} %param.16) | copy-start | bytes 4718596
  0.0 2.9 %copy-start.5 = (s32[3]{0:T(128)S(1)}, s32[3]{0:T(128)}, u32[]{:S(2)}) copy-start(s32[3]{0:T(128)} %param.18) | copy-start | bytes 40
  0.0 3.0 %copy-start.7 = (bf16[3,64,64]{2,1,0:T(8,128)(2,1)S(1)}, bf16[3,64,64]{2,1,0:T(8,128)(2,1)}, u32[]{:S(2)}) copy-start(bf16[3,64,64]{2,1,0:T(8,128)(2,1)} %param.15) | copy-start | bytes 73732
  0.0 3.0 %copy-start.6 = (bf16[3,512,64]{1,2,0:T(8,128)(2,1)S(1)}, bf16[3,512,64]{1,2,0:T(8,128)(2,1)}, u32[]{:S(2)}) copy-start(bf16[3,512,64]{1,2,0:T(8,128)(2,1)} %param.17) | copy-start | bytes 589828
  4.9 31.9 %copy-start.3 = (f32[3,2]{0,1:T(2,128)S(1)}, f32[3,2]{0,1:T(2,128)}, u32[]{:S(2)}) copy-start(f32[3,2]{0,1:T(2,128)} %param.22) | copy-start | bytes 76
  4.9 31.9 %copy-start.4 = (s32[3,2]{0,1:T(2,128)S(1)}, s32[3,2]{0,1:T(2,128)}, u32[]{:S(2)}) copy-start(s32[3,2]{0,1:T(2,128)} %param.21) | copy-start | bytes 76
  4.9 32.7 %copy-start.1 = (bf16[3,7168]{1,0:T(4,128)(2,1)S(1)}, bf16[3,7168]{1,0:T(4,128)(2,1)}, u32[]{:S(2)}) copy-start(bf16[3,7168]{1,0:T(4,128)(2,1)} %param.13) | copy-start | bytes 129028
  4.9 33.4 %copy-start.2 = (f32[7168]{0:T(1024)S(1)}, f32[7168]{0:T(1024)}, u32[]{:S(2)}) copy-start(f32[7168]{0:T(1024)} %param.20) | copy-start | bytes 86020
